TPU v7x, 256 devices: a whole 4x4x8 slice. The times are simulated.
256 devices in a mesh: ctx: 64 (over z, y_hi, x), head: 4 (over y_lo, core).
Axes of the slice: x: 4, y: 4 (y_hi: 2, y_lo: 2; y = y_hi * 2 + y_lo), z: 8, core: 2. Of those that a mesh axis runs over, the one named last changes fastest.
Arguments:
- lin_query: bfloat16 [24576, 8192], P('ctx', 'head'), may hold values from -600 to 600
- lin_key: bfloat16 [24576, 8192], P('ctx', 'head'), may hold values from -6 to 6
- lin_value: bfloat16 [24576, 8192], P('ctx', 'head'), may hold values from -6 to 6
- log_decay: float32 [64, 24576], P('head', 'ctx'), may hold values from -1 to 0
- soft_query: bfloat16 [24576, 8192], P('ctx', 'head'), may hold values from -300 to 300
- soft_key: bfloat16 [24576, 8192], P('ctx', 'head'), may hold values from -6 to 6
- soft_value: bfloat16 [24576, 8192], P('ctx', 'head'), may hold values from -6 to 6
Outputs:
- linear_out: bfloat16 [24576, 8192], P('ctx', 'head')
- window_out: bfloat16 [24576, 8192], P('ctx', 'head')
All inputs are finite; a program needn't handle non-finite values.
Results may differ from a plain program's by a relative error of at most 0.011.
Values may be sent and summed in bfloat16 or wider, within the bound.
A program may use at most 192 MiB of HBM per device.

v0:
```python
import jax
import jax.numpy as jnp
from jax import lax
from jax.sharding import PartitionSpec as P

DH = 128


def carried_in(array, axis, combine, identity):
    count, index = (lax.axis_size(axis), lax.axis_index(axis))
    everything = jax.tree.map(lambda part: lax.all_gather(part, axis), array)
    start = jax.tree.map(
        lambda part, zero: jnp.broadcast_to(jnp.asarray(zero, part.dtype), part.shape),
        array,
        identity,
    )

    def lap(k, before):
        reached = k < index
        new = combine(before, jax.tree.map(lambda part: part[k], everything))
        return jax.tree.map(lambda a, b: jnp.where(reached, a, b), new, before)

    return lax.fori_loop(0, count, lap, start)


def shifted(block, axis, distance):
    devices = range(lax.axis_size(axis))
    route = [(i - distance, i) for i in devices if i - distance in devices]
    return lax.ppermute(block, axis, route)


def follow(earlier, later):
    return (earlier[0] + later[0], jnp.exp(later[0])[:, None, None] * earlier[1] + later[1])


def body(lin_query, lin_key, lin_value, log_decay, soft_query, soft_key, soft_value):
    tok_rows = lin_query.shape[0]
    head_count = log_decay.shape[0]
    queries = lin_query.reshape(tok_rows, head_count, DH)
    key_rows = lin_key.reshape(tok_rows, head_count, DH)
    value_rows = lin_value.reshape(tok_rows, head_count, DH)
    cumulative = jnp.cumsum(log_decay, axis=1)
    block_total = cumulative[:, -1]
    positions = jnp.arange(tok_rows, dtype=jnp.int32)
    causal = positions[:, None] >= positions[None, :]
    decayed = (key_rows * jnp.exp(block_total[:, None] - cumulative).T[:, :, None]).astype(
        jnp.bfloat16
    )
    local_state = jnp.einsum(
        "shd,she->hde", decayed, value_rows, preferred_element_type=jnp.float32
    )
    identity = (jnp.zeros((head_count,), jnp.float32), jnp.zeros((head_count, DH, DH), jnp.float32))
    carried = carried_in((block_total, local_state), "ctx", follow, identity)
    prefix = carried[1]
    decay_mask = jnp.exp(
        jnp.where(causal[None], cumulative[:, :, None] - cumulative[:, None, :], -jnp.inf)
    )
    scores = jnp.einsum("thd,shd->hts", queries, key_rows, preferred_element_type=jnp.float32)
    weights = (scores * decay_mask).astype(jnp.bfloat16)
    inside_part = jnp.einsum(
        "hts,shd->thd", weights, value_rows, preferred_element_type=jnp.float32
    )
    carried_part = jnp.einsum(
        "thd,hde->the", queries.astype(jnp.float32), prefix, precision=lax.Precision.HIGHEST
    )
    combined = inside_part + carried_part * jnp.exp(cumulative).T[:, :, None]
    own_squares = jnp.sum(combined * combined, axis=(1, 2))
    feature_sum = lax.psum(own_squares, "head")
    width_all = head_count * lax.axis_size("head") * DH
    inverse_rms = lax.rsqrt(feature_sum / width_all + 1e-05)
    linear_out = (
        (combined * inverse_rms[:, None, None])
        .reshape(tok_rows, head_count * DH)
        .astype(jnp.bfloat16)
    )
    linear_wide = linear_out.astype(jnp.float32)
    window_query = (soft_query.astype(jnp.float32) + linear_wide).astype(jnp.bfloat16)
    window_value = (soft_value.astype(jnp.float32) + linear_wide).astype(jnp.bfloat16)
    pair_keys = jnp.stack([soft_key, window_value])
    previous = shifted(pair_keys, "ctx", 1)
    before_that = shifted(pair_keys, "ctx", 2)
    key_span = jnp.concatenate([before_that[0], previous[0], soft_key], axis=0)
    value_span = jnp.concatenate([before_that[1], previous[1], window_value], axis=0)
    cycle_place = lax.axis_index("ctx")
    q_pos = cycle_place * tok_rows + jnp.arange(tok_rows, dtype=jnp.int32)
    k_pos = (cycle_place - 2) * tok_rows + jnp.arange(3 * tok_rows, dtype=jnp.int32)
    allowed = (
        (k_pos[None, :] >= 0)
        & (k_pos[None, :] <= q_pos[:, None])
        & (q_pos[:, None] - k_pos[None, :] <= 2 * tok_rows)
    )
    score_scale = DH ** (-0.5)

    def one_head(head_pos, result):
        column = head_pos * DH
        q_part = lax.dynamic_slice_in_dim(window_query, column, DH, 1)
        k_part = lax.dynamic_slice_in_dim(key_span, column, DH, 1)
        v_part = lax.dynamic_slice_in_dim(value_span, column, DH, 1)
        head_scores = (
            lax.dot_general(
                q_part, k_part, (((1,), (1,)), ((), ())), preferred_element_type=jnp.float32
            )
            * score_scale
        )
        head_scores = jnp.where(allowed, head_scores, -jnp.inf)
        row_max = jnp.max(head_scores, axis=-1, keepdims=True)
        raised = jnp.exp(head_scores - row_max)
        probability = (raised / jnp.sum(raised, axis=-1, keepdims=True)).astype(jnp.bfloat16)
        head_out = jnp.dot(probability, v_part, preferred_element_type=jnp.float32).astype(
            jnp.bfloat16
        )
        return lax.dynamic_update_slice_in_dim(result, head_out, column, 1)

    window_out = lax.fori_loop(
        0, head_count, one_head, jnp.zeros((tok_rows, head_count * DH), jnp.bfloat16)
    )
    return (linear_out, window_out)


def solution(mesh):
    placed = (
        P("ctx", "head"),
        P("ctx", "head"),
        P("ctx", "head"),
        P("head", "ctx"),
        P("ctx", "head"),
        P("ctx", "head"),
        P("ctx", "head"),
    )
    return jax.shard_map(
        body,
        mesh=mesh,
        in_specs=placed,
        out_specs=(P("ctx", "head"), P("ctx", "head")),
        check_vma=False,
    )
```

profile of v0, /device:TPU:32, one launch (start us, length us, event | category | flops | bytes accessed | tf_op | source)
XLA Modules:
  0.0 932.0 jit_solution(8380091335368733960)
XLA Ops:
  9.5 1.9 copy.53
  11.4 3.5 fusion.23
  16.4 169.0 %all-reduce = f32[1024]{0:T(1024)S(1)} all-reduce(f32[1024]{0:T(1024)S(1)} %dynamic-update-slice), channel_id=2, replica_groups=mesh['ctx'=64,'head'=4] {'ctx'}, use_global_device_ids=true, to_apply=%add | all-reduce | flops 1024 | bytes 8192
  185.5 403.6 %all-gather.4.cloned.1.call-done = f32[1024,128,128]{2,1,0:T(8,128)} async-done(((f32[16,128,128]{2,1,0:T(8,128)}), f32[1024,128,128]{2,1,0:T(8,128)}) %all-gather.4.cloned.1.call-update) | async-done | bytes 67108880 | tf_op jit(solution)/shard_map/all_gather | solution.py:11
  589.1 96.0 %while.29 = (s32[]{:T(128)}, f32[16,128,128]{2,1,0:T(8,128)S(1)}, s32[]{:T(128)}, f32[64,16]{1,0:T(8,128)S(1)}, f32[64,16,128,128]{3,2,1,0:T(8,128)}, /*index=5*/s32[]{:T(128)}, s32[]{:T(128)}) while((s32[]{:T(128)}, f32[16,128,128]{2,1,0:T(8,128)S(1)}, s32[]{:T(128)}, f32[64,16]{1,0:T(8,128)S(1)}, f32[64,16,128,128]{3,2,1,0:T(8,128)}, ...), condition=%wide.region_3.4_spmd.clone, body=%wide.region_2.3_spmd.clone.sunk | while | flops 1048580 | bytes 3146025 | solution.py:23
  685.2 3.5 fusion.26
  688.7 7.1 multiply_reduce_fusion
  695.8 6.0 psum.7
  701.8 2.2 multiply_convert_fusion.2
  704.0 1.6 copy.51
  705.6 4.7 fusion.21
  710.3 1.9 pad_maximum_fusion.2
  712.3 4.9 collective-permute-start
  717.2 2.5 collective-permute-start.1
  719.7 69.7 %collective-permute-done = bf16[2,384,2048]{2,1,0:T(8,128)(2,1)} collective-permute-done((bf16[2,384,2048]{2,1,0:T(8,128)(2,1)}, bf16[2,384,2048]{2,1,0:T(8,128)(2,1)}, u32[]{:S(2)}, u32[]{:S(2)}) %collective-permute-start) | collective-permute-done | bytes 3145760 | tf_op jit(solution)/shard_map/ppermute | solution.py:29
  789.4 2.1 slice_bitcast_fusion.1
  791.5 65.3 %collective-permute-done.1 = bf16[2,384,2048]{2,1,0:T(8,128)(2,1)} collective-permute-done((bf16[2,384,2048]{2,1,0:T(8,128)(2,1)}, bf16[2,384,2048]{2,1,0:T(8,128)(2,1)}, u32[]{:S(2)}, u32[]{:S(2)}) %collective-permute-start.1) | collective-permute-done | bytes 3145760 | tf_op jit(solution)/shard_map/ppermute | solution.py:29
  856.8 2.1 slice_bitcast_fusion
  859.0 4.5 pad_maximum_fusion
  863.6 60.3 %while.28 = (s32[]{:T(128)}, bf16[384,2048]{1,0:T(8,128)(2,1)S(1)}, bf16[384,2048]{1,0:T(8,128)(2,1)}, bf16[1152,2048]{1,0:T(8,128)(2,1)}, bf16[1152,2048]{1,0:T...) while((s32[]{:T(128)}, bf16[384,2048]{1,0:T(8,128)(2,1)S(1)}, ...), condition=%wide.region_9.10_spmd.clone, body=%wide.region_6.9_spmd.clone.sunk | while | flops 232291584 | bytes 6113059 | solution.py:114
  863.6 1.9 fusion.53
  865.9 1.5 fusion.55
  867.4 1.9 fusion.53
  871.2 1.9 fusion.53
  873.5 1.5 fusion.55
  875.0 1.9 fusion.53
  877.2 1.5 fusion.55
  878.7 1.9 fusion.53
  881.0 1.5 fusion.55
  882.5 1.9 fusion.53
  884.8 1.5 fusion.55
  886.3 1.9 fusion.53
  888.6 1.5 fusion.55
  890.0 1.9 fusion.53
  892.3 1.5 fusion.55
  893.8 1.9 fusion.53
  896.1 1.5 fusion.55
  897.6 1.9 fusion.53
  899.9 1.5 fusion.55
  901.4 1.9 fusion.53
  903.6 1.5 fusion.55
  905.1 1.9 fusion.53
  907.4 1.5 fusion.55
  908.9 1.9 fusion.53
  911.2 1.5 fusion.55
  912.7 1.9 fusion.53
  916.4 1.9 fusion.53
  920.2 1.9 fusion.53
  (180 shorter events, 111.1 us)
Async XLA Ops:
  7.2 678.0 %copy-start = (bf16[384,2048]{1,0:T(8,128)(2,1)S(1)}, bf16[384,2048]{1,0:T(8,128)(2,1)}, u32[]{:S(2)}) copy-start(bf16[384,2048]{1,0:T(8,128)(2,1)} %param.11) | copy-start | bytes 4718596
  7.2 582.0 %all-gather.4.cloned.1.call-start = ((), (), s32[]{:S(2)}) async-start(), calls=%async_computation | async-start | bytes 68157440 | tf_op jit(solution)/shard_map/all_gather | solution.py:11
  11.4 3.6 copy-start.3
  11.4 3.6 copy-start.5
  705.6 4.7 copy-start.1
  712.3 77.1 %collective-permute-start = (bf16[2,384,2048]{2,1,0:T(8,128)(2,1)}, bf16[2,384,2048]{2,1,0:T(8,128)(2,1)}, u32[]{:S(2)}, u32[]{:S(2)}) collective-permute-start(bf16[2,384,2048]{2,1,0:T(8,128)(2,1)} %pad_maximum_fusion.2), channel_id=1, source_target_pairs={{0,8},{4,12},{8,16},{12,20},{16,24},{20,28},{24,32},{28,36},{32,40... | collective-permute-start | bytes 9437192 | tf_op jit(solution)/shard_map/ppermute | solution.py:29
  717.2 139.7 %collective-permute-start.1 = (bf16[2,384,2048]{2,1,0:T(8,128)(2,1)}, bf16[2,384,2048]{2,1,0:T(8,128)(2,1)}, u32[]{:S(2)}, u32[]{:S(2)}) collective-permute-start(bf16[2,384,2048]{2,1,0:T(8,128)(2,1)} %pad_maximum_fusion.2), channel_id=1, source_target_pairs={{0,4},{4,8},{8,12},{12,16},{16,20},{20,24},{24,28},{28,32},{32,36}... | collective-permute-start | bytes 9437192 | tf_op jit(solution)/shard_map/ppermute | solution.py:29
  791.5 67.5 %copy-start.2 = (bf16[384,2048]{1,0:T(8,128)(2,1)S(1)}, bf16[384,2048]{1,0:T(8,128)(2,1)}, u32[]{:S(2)}) copy-start(bf16[384,2048]{1,0:T(8,128)(2,1)} %param.16) | copy-start | bytes 4718596
  924.0 1.1 copy-start.4
Sparse Core Ops, SparseCore 0:
  15.1 574.0 all-gather.3
where the time goes:
time: 936 us; the launch traced here: 932 us
  waiting for transfers between devices  539 us (58%)
  blocking collectives  175 us (19%)
  other arithmetic  114 us (12%)
  matrix products  67.4 us (7%)
  between operations  14.8 us (2%)
  local copies, waits for them, and re-layouts  11.9 us (1%)
    all_gather x1, waiting for transfers between devices, carried_in(): everything = jax.tree.map(lambda part: lax.all_gather(part, axis), array)  404 us
    unnamed x1, blocking collectives  169 us
    ppermute x2, waiting for transfers between devices, shifted(): return lax.ppermute(block, axis, route)  135 us
    select_n x64, other arithmetic, lap(): return jax.tree.map(lambda a, b: jnp.where(reached, a, b), new, before)  93.3 us
    dot_general x16, matrix products, one_head(): lax.dot_general(q_part, k_part, (((1,), (1,)), ((), ())), preferred_eleme...  29.9 us
    dot_general x16, matrix products, one_head(): jnp.dot(probability, v_part, preferred_element_type=jnp.float32)  23.4 us
  transfers between devices with their start and end apart: 3, of which 3 were waited for; matrix products, arithmetic and copies ran while one was open for 0% of the time, Pallas kernels for 0%

commit v1 on v0

v1 whole, which is shorter than its diff:
```python
import jax
import jax.numpy as jnp
from jax import lax
from jax.experimental import pallas as pl
from jax.experimental.pallas import tpu as pltpu
from jax.sharding import PartitionSpec as P

MESH = pl.DeviceIdType.MESH
F32, BF16 = jnp.float32, jnp.bfloat16
DH = 128
H = 16
TOK = 384
NX = 4
NR = 16
NHEAD = 4
G = H // NX
WIN = 768
LINE = NX * TOK
SPAN = WIN + LINE
QT = 128
KT = WIN + QT
EARLY = (True, True, False, False)
LOG2E = 1.4426950408889634


def nt(a, b, **kw):
    return lax.dot_general(a, b, (((1,), (1,)), ((), ())), preferred_element_type=F32, **kw)


def tn(a, b):
    return lax.dot_general(a, b, (((0,), (0,)), ((), ())), preferred_element_type=F32)


def nn(a, b):
    return jnp.dot(a, b, preferred_element_type=F32)


def kernel(
    lq, lk, lv, ld, sq, sk, sv, lin_out, win_out,
    vq, vk, vv, lsq, lsv, lout, cumrow, colb, inside, acc,
    tot, totx, rowtot, rowtots, st, sx, tsrc, trows, pout, prow, px, pre,
    sqs, sqr, kb, vb, qb, lb, ob,
    load, tsem, rtsem, ssem, trsem, psem, xsem, qsem,
    ksem, khsem, vhsem, aqsem, avsem, losem, osem, osend,
):
    c = lax.axis_index("ctx")
    h = lax.axis_index("head")
    r, x = lax.div(c, NX), lax.rem(c, NX)

    def line(k):
        return lax.rem(x + k, NX)

    def row(k):
        return lax.rem(r + k, NR)

    def xdev(k):
        return (r * NX + line(k), h)

    def rdev(k):
        return (row(k) * NX + x, h)

    def hdev(k):
        return (c, lax.rem(h + k, NHEAD))

    def remote(src, dst, sems, dev):
        pltpu.make_async_remote_copy(
            src_ref=src, dst_ref=dst, send_sem=sems.at[0], recv_sem=sems.at[1],
            device_id=dev, device_id_type=MESH,
        ).start()

    def local(src, dst, sem):
        pltpu.make_async_copy(src, dst, sem).start()

    def drain(ref, sem):
        pltpu.make_async_copy(ref, ref, sem).wait()

    def cols(head):
        return pl.ds(pl.multiple_of(head * DH, DH), DH)

    def at_line(k, base=0):
        return pl.ds(pl.multiple_of(base + k * TOK, TOK), TOK)

    barrier = pltpu.get_barrier_semaphore()
    for k in range(1, NX):
        pl.semaphore_signal(barrier, inc=1, device_id=xdev(k), device_id_type=MESH)
    for k in range(1, NHEAD):
        pl.semaphore_signal(barrier, inc=1, device_id=hdev(k), device_id_type=MESH)

    def greet(k, carry):
        pl.semaphore_signal(barrier, inc=1, device_id=rdev(k), device_id_type=MESH)
        return carry

    lax.fori_loop(1, NR, greet, 0)

    local(lk, vk, load.at[0])
    local(lv, vv, load.at[1])
    local(lq, vq, load.at[2])
    for j in range(G):
        own = cols(x * G + j)
        local(sk.at[:, own], kb.at[j, at_line(x, WIN)], load.at[3])
        if EARLY[j]:
            local(sq.at[:, own], qb.at[j, at_line(x)], load.at[4])
            local(sv.at[:, own], vb.at[j, at_line(x, WIN)], load.at[4])
    if not all(EARLY):
        local(sq, lsq, load.at[5])
        local(sv, lsv, load.at[6])

    decay = ld[...]
    at_row = lax.broadcasted_iota(jnp.int32, (TOK, TOK), 0)
    at_col = lax.broadcasted_iota(jnp.int32, (TOK, TOK), 1)
    lower = jnp.where(at_row >= at_col, 1.0, 0.0).astype(F32)
    cumrow[...] = nt(decay, lower, precision=lax.Precision.HIGHEST)
    cum_col = nt(lower, decay, precision=lax.Precision.HIGHEST)
    for hh in range(H):
        colb[hh] = jnp.broadcast_to(cum_col[:, hh : hh + 1], (TOK, DH))
    tot[...] = jnp.broadcast_to(jnp.sum(decay, axis=1, keepdims=True), (H, DH))
    totx[x] = tot[...]

    pl.semaphore_wait(barrier, (NX - 1) + (NHEAD - 1) + (NR - 1))
    for k in range(1, NX):
        remote(tot, totx.at[x], tsem, xdev(k))

    def send_keys(j):
        for k in range(1, NX):
            remote(
                sk.at[:, cols(line(k) * G + j)], kb.at[j, at_line(x, WIN)], ksem.at[j], xdev(k)
            )

    send_keys(0)

    drain(vk, load.at[0])
    drain(vv, load.at[1])

    def state(hh, carry):
        k = vk[:, cols(hh)].astype(F32)
        fall = jnp.exp(tot[pl.ds(hh, 1), :] - colb[hh])
        st[hh] = tn((k * fall).astype(BF16), vv[:, cols(hh)]).astype(BF16)
        return carry

    for k in (2, 1, 3, 0):
        first = line(k) * G
        lax.fori_loop(first, first + G, state, 0)
        if k:
            remote(st.at[pl.ds(first, G)], sx.at[x], ssem, xdev(k))
    sx[x] = st[pl.ds(x * G, G)]

    drain(totx.at[pl.ds(0, NX - 1)], tsem.at[1])
    rowtot[...] = totx[0] + totx[1] + totx[2] + totx[3]
    rowtots[r] = rowtot[...]

    def send_rowtot(k, carry):
        remote(rowtot, rowtots.at[r], rtsem, rdev(k))
        return carry

    lax.fori_loop(1, NR, send_rowtot, 0)

    drain(vq, load.at[2])
    tri = lax.broadcasted_iota(jnp.int32, (QT, QT), 0) >= lax.broadcasted_iota(
        jnp.int32, (QT, QT), 1
    )

    def intra(hh, carry):
        q, k, v = vq[:, cols(hh)], vk[:, cols(hh)], vv[:, cols(hh)]
        crow = cumrow[pl.ds(hh, 1), :]
        for i in range(TOK // QT):
            n = (i + 1) * QT
            scores = nt(q[i * QT : n], k[:n])
            cc = colb[hh, i * QT : n, :]
            parts = []
            for s in range(i + 1):
                gap = cc - crow[:, s * QT : (s + 1) * QT]
                if s == i:
                    gap = jnp.where(tri, gap, -jnp.inf)
                parts.append((scores[:, s * QT : (s + 1) * QT] * jnp.exp(gap)).astype(BF16))
            weights = jnp.concatenate(parts, axis=1) if i else parts[0]
            inside[hh, i * QT : n, :] = nn(weights, v[:n])
        colb[hh] = jnp.exp(colb[hh])
        return carry

    lax.fori_loop(0, H, intra, 0)

    drain(sx.at[pl.ds(0, NX - 1)], ssem.at[1])

    def line_sum(g, carry):
        total = jnp.zeros((DH, DH), F32)
        for s in range(NX):
            total = jnp.exp(totx[s, pl.ds(x * G + g, 1), :]) * total + sx[s, g].astype(F32)
        tsrc[pl.ds(g * 4, 4)] = total.astype(BF16).reshape(4, DH // 4, DH)
        return carry

    lax.fori_loop(0, G, line_sum, 0)
    trows[r] = tsrc[r]

    def send_sum(k, carry):
        remote(tsrc.at[row(k)], trows.at[r], trsem, rdev(k))
        return carry

    lax.fori_loop(1, NR, send_sum, 0)
    for j in range(1, G):
        send_keys(j)

    drain(rowtots.at[pl.ds(0, NR - 1)], rtsem.at[1])
    drain(trows.at[pl.ds(0, NR - 1)], trsem.at[1])
    mine = x * G + lax.div(r, 4)

    def scan_rows(k, before):
        pout[k] = before.astype(BF16)
        return jnp.exp(rowtots[k, pl.ds(mine, 1), :]) * before + trows[k].astype(F32)

    lax.fori_loop(0, NR, scan_rows, jnp.zeros((DH // 4, DH), F32))
    prow[r] = pout[r]

    def send_before(k, carry):
        remote(pout.at[row(k)], prow.at[r], psem, rdev(k))
        return carry

    lax.fori_loop(1, NR, send_before, 0)
    drain(prow.at[pl.ds(0, NR - 1)], psem.at[1])

    def line_scan(g, carry):
        before = prow[pl.ds(g * 4, 4)].reshape(DH, DH).astype(F32)
        for s in range(NX):
            px[s, g] = before.astype(BF16)
            before = jnp.exp(totx[s, pl.ds(x * G + g, 1), :]) * before + sx[s, g].astype(F32)
        return carry

    lax.fori_loop(0, G, line_scan, 0)
    for k in (2, 1, 3):
        remote(px.at[line(k)], pre.at[pl.ds(x * G, G)], xsem, xdev(k))
    pre[pl.ds(x * G, G)] = px[x]

    for j in range(G):
        if EARLY[j]:
            for k in range(1, NX):
                other = cols(line(k) * G + j)
                remote(sv.at[:, other], vb.at[j, at_line(x, WIN)], avsem.at[j], xdev(k))
                remote(sq.at[:, other], qb.at[j, at_line(x)], aqsem.at[j], xdev(k))

    drain(kb.at[pl.ds(0, G), pl.ds(0, TOK)], load.at[3])
    for j in range(G):
        drain(kb.at[j, pl.ds(0, (NX - 1) * TOK)], ksem.at[j, 1])
        remote(kb.at[j, pl.ds(LINE, WIN)], kb.at[j, pl.ds(0, WIN)], khsem.at[j], rdev(1))

    acc[...] = jnp.zeros_like(acc)
    drain(pre.at[pl.ds(0, (NX - 1) * G)], xsem.at[1])

    def carry_in(hh, carry):
        both = inside[hh] + nn(vq[:, cols(hh)], pre[hh]) * colb[hh]
        inside[hh] = both
        acc[...] += both * both
        return carry

    lax.fori_loop(0, H, carry_in, 0)
    eye = at_row == at_col
    squares = jnp.sum(acc[...], axis=1, keepdims=True)
    as_row = jnp.sum(jnp.where(eye, squares, 0.0), axis=0, keepdims=True)
    sqs[...] = jnp.broadcast_to(as_row, sqs.shape)
    for k in range(1, NHEAD):
        remote(sqs, sqr.at[h], qsem, hdev(k))
    sqr[h] = sqs[...]
    if not all(EARLY):
        drain(lsq, load.at[5])
        drain(lsv, load.at[6])
    drain(sqr.at[pl.ds(0, NHEAD - 1)], qsem.at[1])
    feature_sum = sqr[0] + sqr[1] + sqr[2] + sqr[3]
    inverse = lax.rsqrt(feature_sum / (NHEAD * H * DH) + 1e-05)[0:1, :]
    as_col = jnp.sum(jnp.where(eye, inverse, 0.0), axis=1, keepdims=True)
    acc[...] = jnp.broadcast_to(as_col, acc.shape)

    for j in range(G):

        def normalize(k, carry):
            at = cols(k * G + j)
            out = (inside[k * G + j] * acc[...]).astype(BF16)
            lout[:, at] = out
            if not EARLY[j]:
                wide = out.astype(F32)
                lsq[:, at] = (lsq[:, at].astype(F32) + wide).astype(BF16)
                lsv[:, at] = (lsv[:, at].astype(F32) + wide).astype(BF16)
            return carry

        lax.fori_loop(0, NX, normalize, 0)
        for k in range(1, NX):
            other = cols(line(k) * G + j)
            if EARLY[j]:
                remote(lout.at[:, other], lb.at[j, at_line(x)], losem.at[j], xdev(k))
            else:
                remote(lsv.at[:, other], vb.at[j, at_line(x, WIN)], avsem.at[j], xdev(k))
                remote(lsq.at[:, other], qb.at[j, at_line(x)], aqsem.at[j], xdev(k))
        own = cols(x * G + j)
        if EARLY[j]:
            lb[j, at_line(x)] = lout[:, own]
        else:
            vb[j, at_line(x, WIN)] = lsv[:, own]
            qb[j, at_line(x)] = lsq[:, own]
    local(lout, lin_out, load.at[7])

    keep_first = jnp.logical_not(tri) | (
        lax.broadcasted_iota(jnp.int32, (QT, QT), 0) == lax.broadcasted_iota(jnp.int32, (QT, QT), 1)
    )
    key_at = lax.broadcasted_iota(jnp.int32, (QT, QT), 1)
    floor = jnp.where(r == 0, WIN, 0)
    scale = DH**-0.5 * LOG2E

    def tile(j, i, halo):
        start = pl.multiple_of(i * QT, QT)
        q = qb[j, pl.ds(start, QT), :]
        scores = nt(q, kb[j, pl.ds(start, KT), :])
        parts = []
        for t in range(KT // QT):
            part = scores[:, t * QT : (t + 1) * QT]
            keep = None
            if t == 0:
                keep = keep_first
            if t == KT // QT - 1:
                keep = tri
            if halo and t < WIN // QT:
                inside_line = key_at + (start + t * QT) >= floor
                keep = inside_line if keep is None else keep & inside_line
            parts.append(part if keep is None else jnp.where(keep, part, -jnp.inf))
        top = parts[0]
        for part in parts[1:]:
            top = jnp.maximum(top, part)
        top = jnp.max(top, axis=1, keepdims=True)
        raised = [jnp.exp2((part - top) * scale) for part in parts]
        whole = raised[0]
        for part in raised[1:]:
            whole = whole + part
        whole = jnp.sum(whole, axis=1, keepdims=True)
        probability = jnp.concatenate([part.astype(BF16) for part in raised], axis=1)
        out = nn(probability, vb[j, pl.ds(start, KT), :])
        ob[j, pl.ds(start, QT), :] = (out / whole).astype(BF16)

    def send_out(j, b):
        at = cols(x * G + j)
        src = ob.at[j, pl.ds(b * TOK, TOK)]

        @pl.when(b != x)
        def _():
            pltpu.make_async_remote_copy(
                src_ref=src, dst_ref=win_out.at[:, at], send_sem=osend.at[0],
                recv_sem=osem.at[0], device_id=(r * NX + b, h), device_id_type=MESH,
            ).start()

        @pl.when(b == x)
        def _():
            local(src, win_out.at[:, at], load.at[8])

    if any(EARLY):
        drain(qb.at[pl.ds(0, 2 * sum(EARLY)), pl.ds(0, TOK)], load.at[4])
    for j in range(G):
        three = kb.at[j, pl.ds(0, (NX - 1) * TOK)]
        drain(three, avsem.at[j, 1])
        drain(three, aqsem.at[j, 1])
        if EARLY[j]:
            drain(three, losem.at[j, 1])
            wide = lb[j].astype(F32)
            vb[j, pl.ds(WIN, LINE)] = (vb[j, pl.ds(WIN, LINE)].astype(F32) + wide).astype(BF16)
            qb[j] = (qb[j].astype(F32) + wide).astype(BF16)
        remote(vb.at[j, pl.ds(LINE, WIN)], vb.at[j, pl.ds(0, WIN)], vhsem.at[j], rdev(1))

        def later(i, carry):
            tile(j, i, False)
            return carry

        def first(i, carry):
            tile(j, i, True)
            return carry

        lax.fori_loop(WIN // QT, LINE // QT, later, 0)
        for b in range(WIN // TOK, NX):
            send_out(j, b)
        halo = kb.at[j, pl.ds(0, WIN)]
        drain(halo, khsem.at[j, 1])
        drain(halo, vhsem.at[j, 1])
        lax.fori_loop(0, WIN // QT, first, 0)
        for b in range(WIN // TOK):
            send_out(j, b)

    drain(lout, load.at[7])
    drain(kb.at[pl.ds(0, G), pl.ds(0, TOK)], load.at[8])
    rest = ob.at[pl.ds(0, NX - 1)]
    drain(rest, osem.at[0])
    drain(rest, osend.at[0])
    drain(totx.at[pl.ds(0, NX - 1)], tsem.at[0])
    drain(rowtots.at[pl.ds(0, NR - 1)], rtsem.at[0])
    drain(sx.at[pl.ds(0, NX - 1)], ssem.at[0])
    drain(trows.at[pl.ds(0, NR - 1)], trsem.at[0])
    drain(prow.at[pl.ds(0, NR - 1)], psem.at[0])
    drain(px.at[pl.ds(0, NX - 1)], xsem.at[0])
    drain(sqr.at[pl.ds(0, NHEAD - 1)], qsem.at[0])
    for j in range(G):
        three = kb.at[j, pl.ds(0, (NX - 1) * TOK)]
        halo = kb.at[j, pl.ds(0, WIN)]
        drain(three, ksem.at[j, 0])
        drain(halo, khsem.at[j, 0])
        drain(halo, vhsem.at[j, 0])
        drain(three, aqsem.at[j, 0])
        drain(three, avsem.at[j, 0])
        if EARLY[j]:
            drain(three, losem.at[j, 0])


def body(lin_query, lin_key, lin_value, log_decay, soft_query, soft_key, soft_value):
    wide = (TOK, H * DH)
    vmem, dma = pltpu.VMEM, pltpu.SemaphoreType.DMA
    hbm = pl.BlockSpec(memory_space=pl.ANY)
    return pl.pallas_call(
        kernel,
        out_shape=[jax.ShapeDtypeStruct(wide, BF16)] * 2,
        in_specs=[hbm] * 3 + [pl.BlockSpec(memory_space=vmem)] + [hbm] * 3,
        out_specs=[hbm, hbm],
        scratch_shapes=[vmem(wide, BF16)] * 6
        + [
            vmem((H, TOK), F32),
            vmem((H, TOK, DH), F32),
            vmem((H, TOK, DH), F32),
            vmem((TOK, DH), F32),
            vmem((H, DH), F32),
            vmem((NX, H, DH), F32),
            vmem((H, DH), F32),
            vmem((NR, H, DH), F32),
            vmem((H, DH, DH), BF16),
            vmem((NX, G, DH, DH), BF16),
            vmem((NR, DH // 4, DH), BF16),
            vmem((NR, DH // 4, DH), BF16),
            vmem((NR, DH // 4, DH), BF16),
            vmem((NR, DH // 4, DH), BF16),
            vmem((NX, G, DH, DH), BF16),
            vmem((H, DH, DH), BF16),
            vmem((8, TOK), F32),
            vmem((NHEAD, 8, TOK), F32),
            vmem((G, SPAN, DH), BF16),
            vmem((G, SPAN, DH), BF16),
            vmem((G, LINE, DH), BF16),
            vmem((G, LINE, DH), BF16),
            vmem((G, LINE, DH), BF16),
            dma((9,)),
        ]
        + [dma((2,))] * 7
        + [dma((G, 2))] * 6
        + [dma((1,)), dma((1,))],
        compiler_params=pltpu.CompilerParams(
            collective_id=1, has_side_effects=True, vmem_limit_bytes=48 * 2**20
        ),
        cost_estimate=pl.CostEstimate(
            flops=6 * 10**9, bytes_accessed=13 * 2**20, transcendentals=10**7
        ),
    )(lin_query, lin_key, lin_value, log_decay, soft_query, soft_key, soft_value)


def solution(mesh):
    spec = P("ctx", "head")
    return jax.shard_map(
        body,
        mesh=mesh,
        in_specs=(spec, spec, spec, P("head", "ctx"), spec, spec, spec),
        out_specs=(spec, spec),
        check_vma=False,
    )
```

time: 936 us -> 117 us (0.12)
  waiting for transfers between devices: 539 us -> 0 us
  blocking collectives: 175 us -> 0 us
  other arithmetic: 114 us -> 0 us
  Pallas kernels: 0 us -> 111 us
  matrix products: 67.4 us -> 0 us
  between operations: 14.8 us -> 0.65 us
    all_gather x1 -> x0, waiting for transfers between devices: 404 us -> none  [carried_in(): everything = jax.tree.map(lambda part: lax.all_gather(part, axis), array)]
    unnamed x1 -> x0, blocking collectives: 169 us -> none
    ppermute x2 -> x0, waiting for transfers between devices: 135 us -> none  [shifted(): return lax.ppermute(block, axis, route)]
    pallas_call x0 -> x1, Pallas kernels: none -> 111 us  [body(): pl.pallas_call(kernel, out_shape=[jax.ShapeDtypeStruct(wide, BF16)] * 2,...]
    select_n x64 -> x0, other arithmetic: 93.3 us -> none  [lap(): return jax.tree.map(lambda a, b: jnp.where(reached, a, b), new, before)]
    dot_general x35 -> x0, matrix products: 67.4 us -> none  [the longest x16 29.9 us: one_head(): lax.dot_general(q_part, k_part, (((1,), (1,)), ((), ())), preferred_eleme...]
  transfers between devices with their start and end apart: 3 -> 0, of which waited for: 3 -> 0; matrix products, arithmetic and copies ran while one was open for 0% -> 0% of each run, Pallas kernels for 0% -> 0%
where the time goes in v1:
time: 117 us; the launch traced here: 116 us
  Pallas kernels  111 us (95%)
  local copies, waits for them, and re-layouts  4.43 us (4%)
    pallas_call x1, Pallas kernels, body(): pl.pallas_call(kernel, out_shape=[jax.ShapeDtypeStruct(wide, BF16)] * 2,...  111 us
    unnamed x6, local copies, waits for them, and re-layouts  4.43 us

profile of v1, /device:TPU:32, one launch (start us, length us, event | category | flops | bytes accessed | tf_op | source)
XLA Modules:
  0.0 115.9 jit_solution(393272690237571664)
XLA Ops:
  0.6 0.0 copy-start
  0.6 1.4 %copy-done = bf16[384,2048]{1,0:T(8,128)(2,1)S(1)} copy-done((bf16[384,2048]{1,0:T(8,128)(2,1)S(1)}, bf16[384,2048]{1,0:T(8,128)(2,1)}, u32[]{:S(2)}) %copy-start) | copy-done | bytes 1572888
  2.0 0.0 copy-start.1
  2.0 0.7 copy-done.1
  2.8 110.8 %shard_map.86 = (bf16[384,2048]{1,0:T(8,128)(2,1)S(1)}, bf16[384,2048]{1,0:T(8,128)(2,1)S(1)}) custom-call(bf16[384,2048]{1,0:T(8,128)(2,1)S(1)} %copy-done, bf16[384,2048]{1,0:T(8,128)(2,1)} %lk.1, bf16[384,2048]{1,0:T(8,128)(2,1)} %lv.1, f32[16,384]{1,0:T(8,128)S(1)} %copy-done.1, bf16[384,2048]{1,0:T(8,128)(2,1)} %sq.1, bf16[384,2048]{1,0:T(8,128)(2,1)} %sk.1, ...), custom_call_target="tpu_custom_call" | custom-call | flops 6000000000 | bytes 13631488 | tf_op jit(solution)/shard_map/pallas_call | solution.py:408
  113.6 1.1 copy.11
  114.8 1.1 copy.12
Async XLA Ops:
  0.6 1.4 %copy-start = (bf16[384,2048]{1,0:T(8,128)(2,1)S(1)}, bf16[384,2048]{1,0:T(8,128)(2,1)}, u32[]{:S(2)}) copy-start(bf16[384,2048]{1,0:T(8,128)(2,1)} %lq.1) | copy-start | bytes 4718596
  2.0 0.7 copy-start.1

commit v2 on v1

--- a/solution.py
+++ b/solution.py
@@ -20,6 +20,9 @@
 QT = 128
 KT = WIN + QT
 EARLY = (True, True, False, False)
+STATES, PAIR, CARRY, TILES = 4, 2, 4, 3
+SPLIT = (6, 4, 4, 2)
+AHEAD = 4
 LOG2E = 1.4426950408889634
 
 
@@ -42,6 +45,7 @@
     sqs, sqr, kb, vb, qb, lb, ob,
     load, tsem, rtsem, ssem, trsem, psem, xsem, qsem,
     ksem, khsem, vhsem, aqsem, avsem, losem, osem, osend,
+    line_in, all_in,
 ):
     c = lax.axis_index("ctx")
     h = lax.axis_index("head")
@@ -74,6 +78,14 @@
     def drain(ref, sem):
         pltpu.make_async_copy(ref, ref, sem).wait()
 
+    def repeat(first, count, step, f):
+        def some(i, carry):
+            for n in range(step):
+                f(first + i * step + n)
+            return carry
+
+        lax.fori_loop(0, count // step, some, 0)
+
     def cols(head):
         return pl.ds(pl.multiple_of(head * DH, DH), DH)
 
@@ -81,16 +93,22 @@
         return pl.ds(pl.multiple_of(base + k * TOK, TOK), TOK)
 
     barrier = pltpu.get_barrier_semaphore()
-    for k in range(1, NX):
-        pl.semaphore_signal(barrier, inc=1, device_id=xdev(k), device_id_type=MESH)
-    for k in range(1, NHEAD):
-        pl.semaphore_signal(barrier, inc=1, device_id=hdev(k), device_id_type=MESH)
-
-    def greet(k, carry):
-        pl.semaphore_signal(barrier, inc=1, device_id=rdev(k), device_id_type=MESH)
-        return carry
-
-    lax.fori_loop(1, NR, greet, 0)
+
+    def signal(sem, dev):
+        pl.semaphore_signal(sem, inc=1, device_id=dev, device_id_type=MESH)
+
+    @pl.when(x != 0)
+    def _():
+        for k in range(1, NX):
+
+            @pl.when(line(k) != 0)
+            def _():
+                signal(barrier, xdev(k))
+
+    @pl.when(x == 0)
+    def _():
+        for k in range(1, NX):
+            signal(barrier, xdev(k))
 
     local(lk, vk, load.at[0])
     local(lv, vv, load.at[1])
@@ -116,7 +134,23 @@
     tot[...] = jnp.broadcast_to(jnp.sum(decay, axis=1, keepdims=True), (H, DH))
     totx[x] = tot[...]
 
-    pl.semaphore_wait(barrier, (NX - 1) + (NHEAD - 1) + (NR - 1))
+    @pl.when(x != 0)
+    def _():
+        pl.semaphore_wait(barrier, NX - 1)
+        signal(line_in, (r * NX, h))
+
+    @pl.when(x == 0)
+    def _():
+        pl.semaphore_wait(line_in, NX - 1)
+        for k in range(1, NHEAD):
+            signal(barrier, hdev(k))
+
+        def greet(k, carry):
+            signal(barrier, rdev(k))
+            return carry
+
+        lax.fori_loop(1, NR, greet, 0)
+
     for k in range(1, NX):
         remote(tot, totx.at[x], tsem, xdev(k))
 
@@ -131,25 +165,38 @@
     drain(vk, load.at[0])
     drain(vv, load.at[1])
 
-    def state(hh, carry):
+    def state(hh):
         k = vk[:, cols(hh)].astype(F32)
         fall = jnp.exp(tot[pl.ds(hh, 1), :] - colb[hh])
         st[hh] = tn((k * fall).astype(BF16), vv[:, cols(hh)]).astype(BF16)
-        return carry
 
     for k in (2, 1, 3, 0):
         first = line(k) * G
-        lax.fori_loop(first, first + G, state, 0)
+        repeat(first, G, STATES, state)
         if k:
             remote(st.at[pl.ds(first, G)], sx.at[x], ssem, xdev(k))
     sx[x] = st[pl.ds(x * G, G)]
+    send_keys(1)
+    send_keys(2)
+    send_keys(3)
 
     drain(totx.at[pl.ds(0, NX - 1)], tsem.at[1])
-    rowtot[...] = totx[0] + totx[1] + totx[2] + totx[3]
-    rowtots[r] = rowtot[...]
+    whole_line = totx[0] + totx[1] + totx[2] + totx[3]
+    rowtot[...] = jnp.broadcast_to(whole_line[:, None, :], rowtot.shape)
+    rowtots[r] = rowtot[x * G + lax.div(r, NR // G)]
+
+    @pl.when(x == 0)
+    def _():
+        pl.semaphore_wait(barrier, (NR - 1) + (NHEAD - 1))
+        for k in range(1, NX):
+            signal(all_in, xdev(k))
+
+    @pl.when(x != 0)
+    def _():
+        pl.semaphore_wait(all_in, 1)
 
     def send_rowtot(k, carry):
-        remote(rowtot, rowtots.at[r], rtsem, rdev(k))
+        remote(rowtot.at[x * G + lax.div(row(k), NR // G)], rowtots.at[r], rtsem, rdev(k))
         return carry
 
     lax.fori_loop(1, NR, send_rowtot, 0)
@@ -159,7 +206,7 @@
         jnp.int32, (QT, QT), 1
     )
 
-    def intra(hh, carry):
+    def intra(hh):
         q, k, v = vq[:, cols(hh)], vk[:, cols(hh)], vv[:, cols(hh)]
         crow = cumrow[pl.ds(hh, 1), :]
         for i in range(TOK // QT):
@@ -175,9 +222,8 @@
             weights = jnp.concatenate(parts, axis=1) if i else parts[0]
             inside[hh, i * QT : n, :] = nn(weights, v[:n])
         colb[hh] = jnp.exp(colb[hh])
-        return carry
-
-    lax.fori_loop(0, H, intra, 0)
+
+    repeat(0, SPLIT[0], PAIR, intra)
 
     drain(sx.at[pl.ds(0, NX - 1)], ssem.at[1])
 
@@ -196,16 +242,14 @@
         return carry
 
     lax.fori_loop(1, NR, send_sum, 0)
-    for j in range(1, G):
-        send_keys(j)
+    repeat(SPLIT[0], SPLIT[1], PAIR, intra)
 
     drain(rowtots.at[pl.ds(0, NR - 1)], rtsem.at[1])
     drain(trows.at[pl.ds(0, NR - 1)], trsem.at[1])
-    mine = x * G + lax.div(r, 4)
 
     def scan_rows(k, before):
         pout[k] = before.astype(BF16)
-        return jnp.exp(rowtots[k, pl.ds(mine, 1), :]) * before + trows[k].astype(F32)
+        return jnp.exp(rowtots[k, 0:1, :]) * before + trows[k].astype(F32)
 
     lax.fori_loop(0, NR, scan_rows, jnp.zeros((DH // 4, DH), F32))
     prow[r] = pout[r]
@@ -215,6 +259,7 @@
         return carry
 
     lax.fori_loop(1, NR, send_before, 0)
+    repeat(SPLIT[0] + SPLIT[1], SPLIT[2], PAIR, intra)
     drain(prow.at[pl.ds(0, NR - 1)], psem.at[1])
 
     def line_scan(g, carry):
@@ -226,7 +271,7 @@
 
     lax.fori_loop(0, G, line_scan, 0)
     for k in (2, 1, 3):
-        remote(px.at[line(k)], pre.at[pl.ds(x * G, G)], xsem, xdev(k))
+        remote(px.at[line(k)], pre.at[pl.ds(x * G, G)], xsem.at[k - 1], xdev(k))
     pre[pl.ds(x * G, G)] = px[x]
 
     for j in range(G):
@@ -241,16 +286,18 @@
         drain(kb.at[j, pl.ds(0, (NX - 1) * TOK)], ksem.at[j, 1])
         remote(kb.at[j, pl.ds(LINE, WIN)], kb.at[j, pl.ds(0, WIN)], khsem.at[j], rdev(1))
 
+    repeat(SPLIT[0] + SPLIT[1] + SPLIT[2], SPLIT[3], PAIR, intra)
     acc[...] = jnp.zeros_like(acc)
-    drain(pre.at[pl.ds(0, (NX - 1) * G)], xsem.at[1])
-
-    def carry_in(hh, carry):
+
+    def carry_in(hh):
         both = inside[hh] + nn(vq[:, cols(hh)], pre[hh]) * colb[hh]
         inside[hh] = both
         acc[...] += both * both
-        return carry
-
-    lax.fori_loop(0, H, carry_in, 0)
+
+    for k in (0, 1, 3, 2):
+        if k:
+            drain(pre.at[pl.ds(0, G)], xsem.at[k - 1, 1])
+        repeat(lax.rem(x + NX - k, NX) * G, G, CARRY, carry_in)
     eye = at_row == at_col
     squares = jnp.sum(acc[...], axis=1, keepdims=True)
     as_row = jnp.sum(jnp.where(eye, squares, 0.0), axis=0, keepdims=True)
@@ -269,7 +316,7 @@
 
     for j in range(G):
 
-        def normalize(k, carry):
+        def normalize(k):
             at = cols(k * G + j)
             out = (inside[k * G + j] * acc[...]).astype(BF16)
             lout[:, at] = out
@@ -277,9 +324,17 @@
                 wide = out.astype(F32)
                 lsq[:, at] = (lsq[:, at].astype(F32) + wide).astype(BF16)
                 lsv[:, at] = (lsv[:, at].astype(F32) + wide).astype(BF16)
-            return carry
-
-        lax.fori_loop(0, NX, normalize, 0)
+
+        repeat(0, NX, 2, normalize)
+        own = cols(x * G + j)
+        if EARLY[j]:
+            lb[j, at_line(x)] = lout[:, own]
+        else:
+            vb[j, at_line(x, WIN)] = lsv[:, own]
+            qb[j, at_line(x)] = lsq[:, own]
+    local(lout, lin_out, load.at[7])
+
+    def send_sums(j):
         for k in range(1, NX):
             other = cols(line(k) * G + j)
             if EARLY[j]:
@@ -287,13 +342,6 @@
             else:
                 remote(lsv.at[:, other], vb.at[j, at_line(x, WIN)], avsem.at[j], xdev(k))
                 remote(lsq.at[:, other], qb.at[j, at_line(x)], aqsem.at[j], xdev(k))
-        own = cols(x * G + j)
-        if EARLY[j]:
-            lb[j, at_line(x)] = lout[:, own]
-        else:
-            vb[j, at_line(x, WIN)] = lsv[:, own]
-            qb[j, at_line(x)] = lsq[:, own]
-    local(lout, lin_out, load.at[7])
 
     keep_first = jnp.logical_not(tri) | (
         lax.broadcasted_iota(jnp.int32, (QT, QT), 0) == lax.broadcasted_iota(jnp.int32, (QT, QT), 1)
@@ -346,36 +394,43 @@
         def _():
             local(src, win_out.at[:, at], load.at[8])
 
+    for j in range(AHEAD):
+        send_sums(j)
     if any(EARLY):
         drain(qb.at[pl.ds(0, 2 * sum(EARLY)), pl.ds(0, TOK)], load.at[4])
-    for j in range(G):
+    def arrive(j):
         three = kb.at[j, pl.ds(0, (NX - 1) * TOK)]
         drain(three, avsem.at[j, 1])
         drain(three, aqsem.at[j, 1])
         if EARLY[j]:
             drain(three, losem.at[j, 1])
+        if j + AHEAD < G:
+            send_sums(j + AHEAD)
+        if EARLY[j]:
             wide = lb[j].astype(F32)
             vb[j, pl.ds(WIN, LINE)] = (vb[j, pl.ds(WIN, LINE)].astype(F32) + wide).astype(BF16)
             qb[j] = (qb[j].astype(F32) + wide).astype(BF16)
         remote(vb.at[j, pl.ds(LINE, WIN)], vb.at[j, pl.ds(0, WIN)], vhsem.at[j], rdev(1))
 
-        def later(i, carry):
-            tile(j, i, False)
-            return carry
-
-        def first(i, carry):
-            tile(j, i, True)
-            return carry
-
-        lax.fori_loop(WIN // QT, LINE // QT, later, 0)
+    def later(j):
+        repeat(WIN // QT, (LINE - WIN) // QT, TILES, lambda i: tile(j, i, False))
         for b in range(WIN // TOK, NX):
             send_out(j, b)
+
+    def first(j):
         halo = kb.at[j, pl.ds(0, WIN)]
         drain(halo, khsem.at[j, 1])
         drain(halo, vhsem.at[j, 1])
-        lax.fori_loop(0, WIN // QT, first, 0)
+        repeat(0, WIN // QT, TILES, lambda i: tile(j, i, True))
         for b in range(WIN // TOK):
             send_out(j, b)
+
+    for j in range(G):
+        arrive(j)
+        later(j)
+        if j:
+            first(j - 1)
+    first(G - 1)
 
     drain(lout, load.at[7])
     drain(kb.at[pl.ds(0, G), pl.ds(0, TOK)], load.at[8])
@@ -387,7 +442,8 @@
     drain(sx.at[pl.ds(0, NX - 1)], ssem.at[0])
     drain(trows.at[pl.ds(0, NR - 1)], trsem.at[0])
     drain(prow.at[pl.ds(0, NR - 1)], psem.at[0])
-    drain(px.at[pl.ds(0, NX - 1)], xsem.at[0])
+    for k in range(NX - 1):
+        drain(px.at[0], xsem.at[k, 0])
     drain(sqr.at[pl.ds(0, NHEAD - 1)], qsem.at[0])
     for j in range(G):
         three = kb.at[j, pl.ds(0, (NX - 1) * TOK)]
@@ -418,8 +474,8 @@
             vmem((TOK, DH), F32),
             vmem((H, DH), F32),
             vmem((NX, H, DH), F32),
-            vmem((H, DH), F32),
-            vmem((NR, H, DH), F32),
+            vmem((H, 8, DH), F32),
+            vmem((NR, 8, DH), F32),
             vmem((H, DH, DH), BF16),
             vmem((NX, G, DH, DH), BF16),
             vmem((NR, DH // 4, DH), BF16),
@@ -437,11 +493,13 @@
             vmem((G, LINE, DH), BF16),
             dma((9,)),
         ]
-        + [dma((2,))] * 7
+        + [dma((2,))] * 5
+        + [dma((NX - 1, 2)), dma((2,))]
         + [dma((G, 2))] * 6
-        + [dma((1,)), dma((1,))],
+        + [dma((1,)), dma((1,))]
+        + [pltpu.SemaphoreType.REGULAR] * 2,
         compiler_params=pltpu.CompilerParams(
-            collective_id=1, has_side_effects=True, vmem_limit_bytes=48 * 2**20
+            collective_id=1, has_side_effects=True, vmem_limit_bytes=60 * 2**20
         ),
         cost_estimate=pl.CostEstimate(
             flops=6 * 10**9, bytes_accessed=13 * 2**20, transcendentals=10**7

time: 117 us -> 106 us (0.906)
  Pallas kernels: 111 us -> 101 us
    pallas_call x1, Pallas kernels: 111 us -> 101 us  [body(): pl.pallas_call(kernel, out_shape=[jax.ShapeDtypeStruct(wide, BF16)] * 2,...]
    unnamed x6 -> x4, local copies, waits for them, and re-layouts: 4.43 us -> 3.99 us
where the time goes in v2:
time: 106 us; the launch traced here: 105 us
  Pallas kernels  101 us (95%)
  local copies, waits for them, and re-layouts  3.99 us (4%)
    pallas_call x1, Pallas kernels, body(): pl.pallas_call(kernel, out_shape=[jax.ShapeDtypeStruct(wide, BF16)] * 2,...  101 us
    unnamed x4, local copies, waits for them, and re-layouts  3.99 us

profile of v2, /device:TPU:32, one launch (start us, length us, event | category | flops | bytes accessed | tf_op | source)
XLA Modules:
  0.0 105.3 jit_solution(15135289267411714950)
XLA Ops:
  0.6 100.7 %shard_map.86 = (bf16[384,2048]{1,0:T(8,128)(2,1)}, bf16[384,2048]{1,0:T(8,128)(2,1)}) custom-call(bf16[384,2048]{1,0:T(8,128)(2,1)} %lq.1, bf16[384,2048]{1,0:T(8,128)(2,1)} %lk.1, bf16[384,2048]{1,0:T(8,128)(2,1)} %lv.1, f32[16,384]{1,0:T(8,128)} %ld.1, bf16[384,2048]{1,0:T(8,128)(2,1)} %sq.1, bf16[384,2048]{1,0:T(8,128)(2,1)} %sk.1, bf16[384,2048]{1,0:T(8,128)(2,1)} %sv.1), custom_call_target="tpu_custom_call" | custom-call | flops 6000000000 | bytes 13631488 | tf_op jit(solution)/shard_map/pallas_call | solution.py:464
  101.3 0.0 copy-start
  101.4 2.8 %copy.11 = bf16[384,2048]{1,0:T(8,128)(2,1)} copy(bf16[384,2048]{1,0:T(8,128)(2,1)} %get-tuple-element.4) | data formatting | bytes 3145728
  104.2 0.0 copy-done
  104.2 1.1 %copy.12 = bf16[384,2048]{1,0:T(8,128)(2,1)} copy(bf16[384,2048]{1,0:T(8,128)(2,1)S(1)} %copy-done) | data formatting | bytes 3145728
Async XLA Ops:
  101.3 2.9 %copy-start = (bf16[384,2048]{1,0:T(8,128)(2,1)S(1)}, bf16[384,2048]{1,0:T(8,128)(2,1)}, u32[]{:S(2)}) copy-start(bf16[384,2048]{1,0:T(8,128)(2,1)} %get-tuple-element.5) | copy-start | bytes 4718596

commit v3 on v2

--- a/solution.py
+++ b/solution.py
@@ -22,7 +22,6 @@
 EARLY = (True, True, False, False)
 STATES, PAIR, CARRY, TILES = 4, 2, 4, 3
 SPLIT = (6, 4, 4, 2)
-AHEAD = 4
 LOG2E = 1.4426950408889634
 
 
@@ -113,6 +112,31 @@
     local(lk, vk, load.at[0])
     local(lv, vv, load.at[1])
     local(lq, vq, load.at[2])
+    @pl.when(x != 0)
+    def _():
+        pl.semaphore_wait(barrier, NX - 1)
+        signal(line_in, (r * NX, h))
+
+    @pl.when(x == 0)
+    def _():
+        pl.semaphore_wait(line_in, NX - 1)
+        for k in range(1, NHEAD):
+            signal(barrier, hdev(k))
+
+        def greet(k, carry):
+            signal(barrier, rdev(k))
+            return carry
+
+        lax.fori_loop(1, NR, greet, 0)
+
+    def send_keys(j):
+        for k in range(1, NX):
+            remote(
+                sk.at[:, cols(line(k) * G + j)], kb.at[j, at_line(x, WIN)], ksem.at[j], xdev(k)
+            )
+
+    send_keys(0)
+
     for j in range(G):
         own = cols(x * G + j)
         local(sk.at[:, own], kb.at[j, at_line(x, WIN)], load.at[3])
@@ -134,33 +158,8 @@
     tot[...] = jnp.broadcast_to(jnp.sum(decay, axis=1, keepdims=True), (H, DH))
     totx[x] = tot[...]
 
-    @pl.when(x != 0)
-    def _():
-        pl.semaphore_wait(barrier, NX - 1)
-        signal(line_in, (r * NX, h))
-
-    @pl.when(x == 0)
-    def _():
-        pl.semaphore_wait(line_in, NX - 1)
-        for k in range(1, NHEAD):
-            signal(barrier, hdev(k))
-
-        def greet(k, carry):
-            signal(barrier, rdev(k))
-            return carry
-
-        lax.fori_loop(1, NR, greet, 0)
-
     for k in range(1, NX):
         remote(tot, totx.at[x], tsem, xdev(k))
-
-    def send_keys(j):
-        for k in range(1, NX):
-            remote(
-                sk.at[:, cols(line(k) * G + j)], kb.at[j, at_line(x, WIN)], ksem.at[j], xdev(k)
-            )
-
-    send_keys(0)
 
     drain(vk, load.at[0])
     drain(vv, load.at[1])
@@ -281,10 +280,20 @@
                 remote(sv.at[:, other], vb.at[j, at_line(x, WIN)], avsem.at[j], xdev(k))
                 remote(sq.at[:, other], qb.at[j, at_line(x)], aqsem.at[j], xdev(k))
 
+    def to_next(part, sems):
+        @pl.when(r < NR - 1)
+        def _():
+            remote(part.at[pl.ds(LINE, WIN)], part.at[pl.ds(0, WIN)], sems, rdev(1))
+
+    @pl.when(r == 0)
+    def _():
+        kb[:, 0:WIN, :] = jnp.zeros((G, WIN, DH), BF16)
+        vb[:, 0:WIN, :] = jnp.zeros((G, WIN, DH), BF16)
+
     drain(kb.at[pl.ds(0, G), pl.ds(0, TOK)], load.at[3])
     for j in range(G):
         drain(kb.at[j, pl.ds(0, (NX - 1) * TOK)], ksem.at[j, 1])
-        remote(kb.at[j, pl.ds(LINE, WIN)], kb.at[j, pl.ds(0, WIN)], khsem.at[j], rdev(1))
+        to_next(kb.at[j], khsem.at[j])
 
     repeat(SPLIT[0] + SPLIT[1] + SPLIT[2], SPLIT[3], PAIR, intra)
     acc[...] = jnp.zeros_like(acc)
@@ -314,6 +323,15 @@
     as_col = jnp.sum(jnp.where(eye, inverse, 0.0), axis=1, keepdims=True)
     acc[...] = jnp.broadcast_to(as_col, acc.shape)
 
+    def send_sums(j):
+        for k in range(1, NX):
+            other = cols(line(k) * G + j)
+            if EARLY[j]:
+                remote(lout.at[:, other], lb.at[j, at_line(x)], losem.at[j], xdev(k))
+            else:
+                remote(lsv.at[:, other], vb.at[j, at_line(x, WIN)], avsem.at[j], xdev(k))
+                remote(lsq.at[:, other], qb.at[j, at_line(x)], aqsem.at[j], xdev(k))
+
     for j in range(G):
 
         def normalize(k):
@@ -326,6 +344,7 @@
                 lsv[:, at] = (lsv[:, at].astype(F32) + wide).astype(BF16)
 
         repeat(0, NX, 2, normalize)
+        send_sums(j)
         own = cols(x * G + j)
         if EARLY[j]:
             lb[j, at_line(x)] = lout[:, own]
@@ -333,15 +352,6 @@
             vb[j, at_line(x, WIN)] = lsv[:, own]
             qb[j, at_line(x)] = lsq[:, own]
     local(lout, lin_out, load.at[7])
-
-    def send_sums(j):
-        for k in range(1, NX):
-            other = cols(line(k) * G + j)
-            if EARLY[j]:
-                remote(lout.at[:, other], lb.at[j, at_line(x)], losem.at[j], xdev(k))
-            else:
-                remote(lsv.at[:, other], vb.at[j, at_line(x, WIN)], avsem.at[j], xdev(k))
-                remote(lsq.at[:, other], qb.at[j, at_line(x)], aqsem.at[j], xdev(k))
 
     keep_first = jnp.logical_not(tri) | (
         lax.broadcasted_iota(jnp.int32, (QT, QT), 0) == lax.broadcasted_iota(jnp.int32, (QT, QT), 1)
@@ -394,8 +404,6 @@
         def _():
             local(src, win_out.at[:, at], load.at[8])
 
-    for j in range(AHEAD):
-        send_sums(j)
     if any(EARLY):
         drain(qb.at[pl.ds(0, 2 * sum(EARLY)), pl.ds(0, TOK)], load.at[4])
     def arrive(j):
@@ -404,13 +412,11 @@
         drain(three, aqsem.at[j, 1])
         if EARLY[j]:
             drain(three, losem.at[j, 1])
-        if j + AHEAD < G:
-            send_sums(j + AHEAD)
         if EARLY[j]:
             wide = lb[j].astype(F32)
             vb[j, pl.ds(WIN, LINE)] = (vb[j, pl.ds(WIN, LINE)].astype(F32) + wide).astype(BF16)
             qb[j] = (qb[j].astype(F32) + wide).astype(BF16)
-        remote(vb.at[j, pl.ds(LINE, WIN)], vb.at[j, pl.ds(0, WIN)], vhsem.at[j], rdev(1))
+        to_next(vb.at[j], vhsem.at[j])
 
     def later(j):
         repeat(WIN // QT, (LINE - WIN) // QT, TILES, lambda i: tile(j, i, False))
@@ -418,9 +424,12 @@
             send_out(j, b)
 
     def first(j):
-        halo = kb.at[j, pl.ds(0, WIN)]
-        drain(halo, khsem.at[j, 1])
-        drain(halo, vhsem.at[j, 1])
+        @pl.when(r > 0)
+        def _():
+            halo = kb.at[j, pl.ds(0, WIN)]
+            drain(halo, khsem.at[j, 1])
+            drain(halo, vhsem.at[j, 1])
+
         repeat(0, WIN // QT, TILES, lambda i: tile(j, i, True))
         for b in range(WIN // TOK):
             send_out(j, b)
@@ -447,10 +456,14 @@
     drain(sqr.at[pl.ds(0, NHEAD - 1)], qsem.at[0])
     for j in range(G):
         three = kb.at[j, pl.ds(0, (NX - 1) * TOK)]
-        halo = kb.at[j, pl.ds(0, WIN)]
         drain(three, ksem.at[j, 0])
-        drain(halo, khsem.at[j, 0])
-        drain(halo, vhsem.at[j, 0])
+
+        @pl.when(r < NR - 1)
+        def _():
+            halo = kb.at[j, pl.ds(0, WIN)]
+            drain(halo, khsem.at[j, 0])
+            drain(halo, vhsem.at[j, 0])
+
         drain(three, aqsem.at[j, 0])
         drain(three, avsem.at[j, 0])
         if EARLY[j]:
@@ -460,7 +473,7 @@
 def body(lin_query, lin_key, lin_value, log_decay, soft_query, soft_key, soft_value):
     wide = (TOK, H * DH)
     vmem, dma = pltpu.VMEM, pltpu.SemaphoreType.DMA
-    hbm = pl.BlockSpec(memory_space=pl.ANY)
+    hbm = pl.BlockSpec(memory_space=pltpu.HBM)
     return pl.pallas_call(
         kernel,
         out_shape=[jax.ShapeDtypeStruct(wide, BF16)] * 2,

time: 106 us -> 106 us (level)
  no operation moved by 1% of the time
where the time goes in v3:
time: 106 us
  Pallas kernels  101 us (95%)
  local copies, waits for them, and re-layouts  3.99 us (4%)
    pallas_call x1, Pallas kernels, body(): pl.pallas_call(kernel, out_shape=[jax.ShapeDtypeStruct(wide, BF16)] * 2,...  101 us
    unnamed x4, local copies, waits for them, and re-layouts  3.99 us

profile of v3, /device:TPU:32, one launch (start us, length us, event | category | flops | bytes accessed | tf_op | source)
XLA Modules:
  0.0 105.6 jit_solution(15396294083367735110)
XLA Ops:
  0.6 100.9 %shard_map.86 = (bf16[384,2048]{1,0:T(8,128)(2,1)}, bf16[384,2048]{1,0:T(8,128)(2,1)}) custom-call(bf16[384,2048]{1,0:T(8,128)(2,1)} %lq.1, bf16[384,2048]{1,0:T(8,128)(2,1)} %lk.1, bf16[384,2048]{1,0:T(8,128)(2,1)} %lv.1, f32[16,384]{1,0:T(8,128)} %ld.1, bf16[384,2048]{1,0:T(8,128)(2,1)} %sq.1, bf16[384,2048]{1,0:T(8,128)(2,1)} %sk.1, bf16[384,2048]{1,0:T(8,128)(2,1)} %sv.1), custom_call_target="tpu_custom_call" | custom-call | flops 6000000000 | bytes 13631488 | tf_op jit(solution)/shard_map/pallas_call | solution.py:477
  101.6 0.0 copy-start
  101.6 2.8 %copy.11 = bf16[384,2048]{1,0:T(8,128)(2,1)} copy(bf16[384,2048]{1,0:T(8,128)(2,1)} %get-tuple-element.4) | data formatting | bytes 3145728
  104.4 0.0 copy-done
  104.4 1.1 %copy.12 = bf16[384,2048]{1,0:T(8,128)(2,1)} copy(bf16[384,2048]{1,0:T(8,128)(2,1)S(1)} %copy-done) | data formatting | bytes 3145728
Async XLA Ops:
  101.6 2.9 %copy-start = (bf16[384,2048]{1,0:T(8,128)(2,1)S(1)}, bf16[384,2048]{1,0:T(8,128)(2,1)}, u32[]{:S(2)}) copy-start(bf16[384,2048]{1,0:T(8,128)(2,1)} %get-tuple-element.5) | copy-start | bytes 4718596

commit v4 on v3

--- a/solution.py
+++ b/solution.py
@@ -179,6 +179,17 @@
     send_keys(2)
     send_keys(3)
 
+    def send_inputs(j):
+        for k in range(1, NX):
+            other = cols(line(k) * G + j)
+            remote(sv.at[:, other], vb.at[j, at_line(x, WIN)], avsem.at[j], xdev(k))
+            remote(sq.at[:, other], qb.at[j, at_line(x)], aqsem.at[j], xdev(k))
+
+    @pl.when(r < NR // 2)
+    def _():
+        send_inputs(0)
+
+
     drain(totx.at[pl.ds(0, NX - 1)], tsem.at[1])
     whole_line = totx[0] + totx[1] + totx[2] + totx[3]
     rowtot[...] = jnp.broadcast_to(whole_line[:, None, :], rowtot.shape)
@@ -274,11 +285,12 @@
     pre[pl.ds(x * G, G)] = px[x]
 
     for j in range(G):
-        if EARLY[j]:
-            for k in range(1, NX):
-                other = cols(line(k) * G + j)
-                remote(sv.at[:, other], vb.at[j, at_line(x, WIN)], avsem.at[j], xdev(k))
-                remote(sq.at[:, other], qb.at[j, at_line(x)], aqsem.at[j], xdev(k))
+        if EARLY[j] and j:
+            send_inputs(j)
+
+    @pl.when(r >= NR // 2)
+    def _():
+        send_inputs(0)
 
     def to_next(part, sems):
         @pl.when(r < NR - 1)

time: 106 us -> 105 us (level)
  the two profiles are of different devices: /device:TPU:32 before, /device:TPU:160 now
where the time goes in v4:
time: 105 us
  Pallas kernels  100 us (95%)
  local copies, waits for them, and re-layouts  3.99 us (4%)
    pallas_call x1, Pallas kernels, body(): pl.pallas_call(kernel, out_shape=[jax.ShapeDtypeStruct(wide, BF16)] * 2,...  100 us
    unnamed x4, local copies, waits for them, and re-layouts  3.99 us

profile of v4, /device:TPU:160, one launch (start us, length us, event | category | flops | bytes accessed | tf_op | source)
XLA Modules:
  0.0 105.0 jit_solution(5785539161236742625)
XLA Ops:
  0.6 100.3 %shard_map.86 = (bf16[384,2048]{1,0:T(8,128)(2,1)}, bf16[384,2048]{1,0:T(8,128)(2,1)}) custom-call(bf16[384,2048]{1,0:T(8,128)(2,1)} %lq.1, bf16[384,2048]{1,0:T(8,128)(2,1)} %lk.1, bf16[384,2048]{1,0:T(8,128)(2,1)} %lv.1, f32[16,384]{1,0:T(8,128)} %ld.1, bf16[384,2048]{1,0:T(8,128)(2,1)} %sq.1, bf16[384,2048]{1,0:T(8,128)(2,1)} %sk.1, bf16[384,2048]{1,0:T(8,128)(2,1)} %sv.1), custom_call_target="tpu_custom_call" | custom-call | flops 6000000000 | bytes 13631488 | tf_op jit(solution)/shard_map/pallas_call | solution.py:489
  100.9 0.0 copy-start
  101.0 2.8 %copy.11 = bf16[384,2048]{1,0:T(8,128)(2,1)} copy(bf16[384,2048]{1,0:T(8,128)(2,1)} %get-tuple-element.4) | data formatting | bytes 3145728
  103.8 0.0 copy-done
  103.8 1.1 %copy.12 = bf16[384,2048]{1,0:T(8,128)(2,1)} copy(bf16[384,2048]{1,0:T(8,128)(2,1)S(1)} %copy-done) | data formatting | bytes 3145728
Async XLA Ops:
  100.9 2.9 %copy-start = (bf16[384,2048]{1,0:T(8,128)(2,1)S(1)}, bf16[384,2048]{1,0:T(8,128)(2,1)}, u32[]{:S(2)}) copy-start(bf16[384,2048]{1,0:T(8,128)(2,1)} %get-tuple-element.5) | copy-start | bytes 4718596
